TPU v7x, 256 devices: a whole 4x4x8 slice. The times are simulated.
256 devices in a mesh: section: 4 (over y_lo, core), patch: 64 (over y_hi, x, z).
Axes of the slice: x: 4, y: 4 (y_hi: 2, y_lo: 2; y = y_hi * 2 + y_lo), z: 8, core: 2. Of those that a mesh axis runs over, the one named last changes fastest.
Arguments:
- timestep: int32 [1], replicated, may hold values from 0 to 999
- stored: bfloat16 [4, 2, 64, 64, 640], P('section', None, 'patch'), may hold values from -60 to 60
- conv_kernel: bfloat16 [4, 3, 3, 640, 640], P('section'), may hold values from -0.078125 to 0.078125
- conv_bias: float32 [4, 640], P('section'), may hold values from -3 to 3
- group_gain: float32 [4, 640], P('section'), may hold values from 0.1 to 1.9
- group_bias: float32 [4, 640], P('section'), may hold values from -3 to 3
- time_weight: bfloat16 [4, 320, 640], P('section'), may hold values from -0.5 to 0.5
- norm_gain: float32 [4, 640], P('section'), may hold values from 0.1 to 1.9
- norm_bias: float32 [4, 640], P('section'), may hold values from -3 to 3
- w_query: bfloat16 [4, 640, 640], P('section'), may hold values from -7.5104094 to 7.5104094
- w_key: bfloat16 [4, 640, 640], P('section'), may hold values from -0.237170825 to 0.237170825
- w_value: bfloat16 [4, 640, 640], P('section'), may hold values from -0.25 to 0.25
- w_out: bfloat16 [4, 640, 640], P('section'), may hold values from -0.25 to 0.25
Outputs:
- fresh: bfloat16 [4, 2, 64, 64, 640], P('section', None, 'patch')
- handed: bfloat16 [4, 2, 64, 64, 640], P('section', None, 'patch')
All inputs are finite; a program needn't handle non-finite values.
Results may differ from a plain program's by a relative error of at most 0.014.
Values may be sent and summed in bfloat16 or wider, within the bound.
A program may use at most 128 MiB of HBM per device.

v0:
```python
import functools
import math

import jax
import jax.numpy as jnp
from jax import lax
from jax.experimental import pallas as pl
from jax.experimental.pallas import tpu as pltpu
from jax.sharding import PartitionSpec as P

GROUPS = 32
HEAD_DIM = 64
HEADS = 10
C = 640
W = 64
H = 64
IMAGES = 2
TEMB = 320
PER = C // GROUPS
LANES = 128
X = 4
Z = 8
GROUP = 16
KEYS = GROUP * W
QB = 256
F32 = jnp.float32
BF16 = jnp.bfloat16


def thirds(value):
    hi = value.astype(BF16).astype(F32)
    mid = (value - hi).astype(BF16).astype(F32)
    lo = (value - hi - mid).astype(BF16).astype(F32)
    return hi, mid, lo


def exact_dot(value, matrix):
    parts = jnp.concatenate([*thirds(value), jnp.zeros_like(value)], axis=0).astype(BF16)
    out = jnp.dot(parts, matrix, preferred_element_type=F32)
    return out[0:8] + out[8:16] + out[16:24]


def rolled(value):
    return pltpu.roll(value, HEAD_DIM, 1)


def lanes_of(shape):
    return lax.broadcasted_iota(jnp.int32, shape, 1)


def kernel(
    ts_hbm, x_hbm, ck_hbm, cb_hbm, gg_hbm, gb_hbm, tw_hbm, ng_hbm, nb_hbm, wq_hbm, wk_hbm, wv_hbm, wo_hbm,
    fresh_hbm, handed_hbm,
    ts_ref, vectors, xin, wc, wt, wq, wk, wv, wo,
    stat_tx, stat_rx, stat2_rx, pad, patches, resid_s,
    send_a, send_b, send_q, recv_a, recv_b, recv_q, kvx, q_main, q_extra,
    m_s, acc_s, part_tx, part_rx, o_tx, o_rx, att, fresh_s,
    x_sem, w_sem, st_send, st_recv, halo_send, halo_recv,
    a_send, a_recv, b_send, b_recv, q_send, q_recv, f_send, f_recv, qf_send, p_send, p_recv, o_send, o_recv,
    out_sem, h_send, h_recv, v_sem,
):
    me = lax.axis_index("patch")
    sec = lax.axis_index("section")
    my_y = me // (X * Z)
    my_x = (me // Z) % X
    my_z = me % Z
    my_i = my_y * Z + my_z

    def at(y, x, z):
        return {"patch": y * (X * Z) + x * Z + z}

    def sent(ref, sem):
        pltpu.make_async_copy(ref, ref, sem).wait()

    x_copy = pltpu.make_async_copy(x_hbm.at[0, :, 0], xin.at[1], x_sem)
    x_copy.start()
    loads = [
        pltpu.make_async_copy(tw_hbm.at[0], wt, w_sem.at[0]),
        pltpu.make_async_copy(ck_hbm.at[0], wc, w_sem.at[1]),
        pltpu.make_async_copy(wq_hbm.at[0], wq, w_sem.at[2]),
        pltpu.make_async_copy(wk_hbm.at[0], wk, w_sem.at[3]),
        pltpu.make_async_copy(wv_hbm.at[0], wv, w_sem.at[4]),
        pltpu.make_async_copy(wo_hbm.at[0], wo, w_sem.at[5]),
    ]
    small = [
        pltpu.make_async_copy(ref, vectors.at[n], v_sem.at[n])
        for n, ref in enumerate((cb_hbm, gg_hbm, gb_hbm, ng_hbm, nb_hbm))
    ]
    small.append(pltpu.make_async_copy(ts_hbm, ts_ref, v_sem.at[5]))
    for load in [*small, *loads]:
        load.start()

    barrier = pltpu.get_barrier_semaphore()

    def greet(device):
        pl.semaphore_signal(barrier, inc=1, device_id=device, device_id_type=pl.DeviceIdType.MESH)

    @pl.loop(1, GROUP)
    def _(k):
        i = (my_i + k) % GROUP
        greet(at(i // Z, my_x, i % Z))

    for k in range(1, X):
        greet(at(my_y, (my_x + k) % X, my_z))
    greet({"patch": (me + 1) % H})
    greet({"patch": (me + H - 1) % H})
    greet({"section": (sec + 1) % 4})
    greet({"section": (sec + 3) % 4})

    channel = lax.broadcasted_iota(jnp.int32, (C, LANES), 0)
    group = lax.broadcasted_iota(jnp.int32, (C, LANES), 1)
    gather = ((channel >= group * PER) & (channel < (group + 1) * PER)).astype(F32).astype(BF16)
    group_t = lax.broadcasted_iota(jnp.int32, (LANES, C), 0)
    channel_t = lax.broadcasted_iota(jnp.int32, (LANES, C), 1)
    spread = ((channel_t >= group_t * PER) & (channel_t < (group_t + 1) * PER)).astype(F32).astype(BF16)
    x_copy.wait()
    mine = xin[1].astype(F32)
    sums = [jnp.sum(mine[b], axis=0, keepdims=True) for b in range(IMAGES)]
    squares = [jnp.sum(mine[b] * mine[b], axis=0, keepdims=True) for b in range(IMAGES)]
    stacked = jnp.concatenate([*sums, *squares, jnp.zeros((4, C), F32)], axis=0)
    own_stats = exact_dot(stacked, gather)
    stat_tx[...] = own_stats
    stat_rx[my_i] = own_stats

    pl.semaphore_wait(barrier, GROUP - 1 + X - 1 + 4)

    @pl.loop(1, GROUP)
    def _(k):
        i = (my_i + k) % GROUP
        pltpu.make_async_remote_copy(
            stat_tx, stat_rx.at[my_i], st_send.at[0], st_recv.at[0], device_id=at(i // Z, my_x, i % Z)
        ).start()

    below = pltpu.make_async_remote_copy(
        xin.at[1], xin.at[0], halo_send.at[0], halo_recv.at[0], device_id={"patch": (me + 1) % H}
    )
    above = pltpu.make_async_remote_copy(
        xin.at[1], xin.at[2], halo_send.at[1], halo_recv.at[1], device_id={"patch": (me + H - 1) % H}
    )
    below.start()
    above.start()

    half = TEMB // 2
    place = lax.broadcasted_iota(jnp.int32, (8, TEMB), 1)
    step = jnp.where(place < half, place, place - half).astype(F32)
    for load in small:
        load.wait()
    angle = ts_ref[0].astype(F32) * jnp.exp(step * (-math.log(10000.0) / half))
    tembed = jnp.where(place < half, jnp.cos(angle), jnp.sin(angle))
    loads[0].wait()
    tproj = exact_dot(tembed * jax.nn.sigmoid(tembed), wt[...])[0:1]
    constant = tproj + vectors[0]

    fifteen = stat_rx.at[pl.ds(0, GROUP - 1)]
    sent(fifteen, st_recv.at[0])
    column_stats = jnp.sum(stat_rx[...], axis=0)
    stat2_rx[my_x] = column_stats
    sent(fifteen, st_send.at[0])
    for k in (1, 3, 2):
        pltpu.make_async_remote_copy(
            stat2_rx.at[my_x], stat2_rx.at[my_x], st_send.at[1], st_recv.at[1],
            device_id=at(my_y, (my_x + k) % X, my_z),
        ).start()
    three = stat2_rx.at[pl.ds(0, X - 1)]
    sent(three, st_recv.at[1])
    stats = jnp.sum(stat2_rx[...], axis=0) * (1.0 / (H * W * PER))
    mean = stats[0:2]
    rstd = lax.rsqrt(stats[2:4] - mean * mean + 1e-05)
    wide = exact_dot(jnp.concatenate([mean, rstd, jnp.zeros((4, LANES), F32)], axis=0), spread)
    scale = wide[2:4] * vectors[1]
    shift = vectors[2] - wide[0:2] * scale

    below.wait_recv()
    above.wait_recv()
    keep = [(me > 0).astype(F32), 1.0, (me < H - 1).astype(F32)]
    edge = jnp.zeros((8, C), F32)
    for b in range(IMAGES):
        for di in range(3):
            line = xin[di, b].astype(F32) * scale[b : b + 1] + shift[b : b + 1]
            line = line * jax.nn.sigmoid(line)
            if di != 1:
                line = line * keep[di]
            pad[b, di, 0:8] = edge
            pad[b, di, 72:80] = edge
            pad[b, di, 8:72] = line
            for dj in range(3):
                tap = di * 3 + dj
                patches[b * W : (b + 1) * W, tap * C : (tap + 1) * C] = pad[b, di, 7 + dj : 71 + dj].astype(BF16)
    loads[1].wait()
    conv = jnp.dot(patches[...], wc[...].reshape(9 * C, C), preferred_element_type=F32)
    resid = (xin[1].astype(F32).reshape(IMAGES * W, C) + conv + constant).astype(BF16)
    resid_s[...] = resid
    r32 = resid.astype(F32)
    centre = jnp.mean(r32, axis=-1, keepdims=True)
    off = r32 - centre
    lvar = jnp.mean(off * off, axis=-1, keepdims=True)
    normed = (off * lax.rsqrt(lvar + 1e-05) * vectors[3] + vectors[4]).astype(BF16)

    left = lanes_of((W, LANES)) < HEAD_DIM
    left_half = lanes_of((W // 2, LANES)) < HEAD_DIM
    for load in loads[2:5]:
        load.wait()
    queries = jnp.dot(normed, wq[...], preferred_element_type=F32) * (HEAD_DIM**-0.5)
    keys = jnp.dot(normed, wk[...], preferred_element_type=F32)
    values = jnp.dot(normed, wv[...], preferred_element_type=F32)
    for b in range(IMAGES):
        rows = slice(b * W, (b + 1) * W)
        for j in range(HEADS // 2):
            lanes = slice(j * LANES, (j + 1) * LANES)
            k_pair, v_pair, q_pair = keys[rows, lanes], values[rows, lanes], queries[rows, lanes]
            top, bottom = q_pair[: W // 2], q_pair[W // 2 :]
            kv = (jnp.where(left, k_pair, rolled(v_pair)), jnp.where(left, rolled(k_pair), v_pair))
            qq = (jnp.where(left_half, top, rolled(bottom)), jnp.where(left_half, rolled(top), bottom))
            for e in range(2):
                head = 2 * j + e
                if head < Z:
                    send_a[b, head, 0:32] = qq[e].astype(BF16)
                    send_a[b, head, 32:96] = kv[e].astype(BF16)
                else:
                    send_q[b, head - Z] = qq[e].astype(BF16)
                    send_b[b, head - Z] = kv[e].astype(BF16)

    def partner(k):
        m = k // 2
        odd = m % 2
        dz = odd * ((m + 1) // 2) + (1 - odd) * ((Z - m // 2) % Z)
        return (my_y + k % 2) % 2, dz

    @pl.loop(0, GROUP)
    def _(k):
        b, dz = partner(k)
        z = (my_z + dz) % Z

        @pl.when(k == 0)
        def _():
            pltpu.make_async_copy(send_a.at[b, z], recv_a.at[my_i], a_recv.at[my_i]).start()

        @pl.when(k > 0)
        def _():
            pltpu.make_async_remote_copy(
                send_a.at[b, z], recv_a.at[my_i], a_send, a_recv.at[my_i], device_id=at(b, my_x, z)
            ).start()

    member = my_y * 2 + my_z % 2
    for b in range(IMAGES):
        for e in range(2):
            z = my_z // 2 + 4 * e
            here = (z == my_z) & (my_y == b)

            @pl.when(here)
            def _():
                pltpu.make_async_copy(send_q.at[b, e], recv_q.at[my_x, member], q_recv.at[my_x]).start()

            @pl.when(jnp.logical_not(here))
            def _():
                pltpu.make_async_remote_copy(
                    send_q.at[b, e], recv_q.at[my_x, member], q_send.at[b * 2 + e], q_recv.at[my_x],
                    device_id=at(b, my_x, z),
                ).start()

    @pl.loop(0, GROUP)
    def _(k):
        b, dz = partner(k)
        z = (my_z + dz) % Z

        @pl.when(k == 0)
        def _():
            pltpu.make_async_copy(send_b.at[b, z // 4], recv_b.at[my_i], b_recv).start()

        @pl.when(k > 0)
        def _():
            pltpu.make_async_remote_copy(
                send_b.at[b, z // 4], recv_b.at[my_i], b_send, b_recv, device_id=at(b, my_x, z)
            ).start()

    @pl.loop(0, GROUP)
    def _(k):
        y, dz = partner(k)
        z = (my_z + Z - dz) % Z
        i = y * Z + z
        sent(recv_a.at[i], a_recv.at[i])
        chunk = recv_a.at[i, pl.ds(32, W)]
        pltpu.make_async_copy(chunk, kvx.at[my_x, i], f_recv.at[my_x]).start()
        for d in (1, 3, 2):
            pltpu.make_async_remote_copy(
                chunk, kvx.at[my_x, i], f_send, f_recv.at[my_x], device_id=at(my_y, (my_x + d) % X, my_z)
            ).start()

    sent(recv_q.at[my_x], q_recv.at[my_x])
    for d in (1, 3, 2):
        pltpu.make_async_remote_copy(
            recv_q.at[my_x], recv_q.at[my_x], qf_send, q_recv.at[my_x],
            device_id=at(my_y, (my_x + d) % X, my_z),
        ).start()

    def unpack(packed, out, base):
        wide = packed.astype(F32)
        out[pl.ds(base, 32)] = jnp.where(left_half, wide, 0.0).astype(BF16)
        out[pl.ds(base + 32, 32)] = jnp.where(left_half, rolled(wide), 0.0).astype(BF16)

    @pl.loop(0, GROUP)
    def _(i):
        unpack(recv_a[i, 0:32], q_main, pl.multiple_of(i * W, W))

    def rows_of(n):
        return slice(n * QB, (n + 1) * QB)

    lane_k = lanes_of((KEYS, LANES))

    def score_of(q, kv):
        return lax.dot_general(q, kv, (((1,), (1,)), ((), ())), preferred_element_type=F32)

    def softened(score, old):
        pieces = [score[:, i * LANES : (i + 1) * LANES] for i in range(KEYS // LANES)]
        top = jnp.max(functools.reduce(jnp.maximum, pieces), axis=-1, keepdims=True)
        top = jnp.broadcast_to(top, (QB, LANES))
        if old is not None:
            top = jnp.maximum(old, top)
        probs = jnp.concatenate([jnp.exp(piece - top).astype(BF16) for piece in pieces], axis=1)
        return top, probs, None if old is None else jnp.exp(old - top)

    def attend(kv, queries, old_tops, old_sums, done):
        ones_values = jnp.where(lane_k < HEAD_DIM, 1.0, kv.astype(F32)).astype(BF16)
        blocks = KEYS // QB
        score = score_of(queries(0), kv)
        for n in range(blocks):
            following = score_of(queries(n + 1), kv) if n + 1 < blocks else None
            top, probs, fade = softened(score, None if old_tops is None else old_tops(n))
            out = jnp.dot(probs, ones_values, preferred_element_type=F32)
            if fade is not None:
                out = out + fade * old_sums(n)
            done(n, top, out)
            score = following

    def keys_of(c):
        return kvx[c].reshape(KEYS, LANES)

    def main_queries(n):
        return q_main[rows_of(n)]

    def main_tops(n):
        return m_s[rows_of(n)]

    def main_sums(n):
        return acc_s[rows_of(n)]

    def keep_main(n, top, out):
        m_s[rows_of(n)] = top
        acc_s[rows_of(n)] = out

    sent(kvx.at[my_x], f_recv.at[my_x])
    attend(keys_of(my_x), main_queries, None, None, keep_main)

    def main_step(d):
        c = (my_x + d) % X
        sent(kvx.at[c], f_recv.at[c])
        attend(keys_of(c), main_queries, main_tops, main_sums, keep_main)

    main_step(1)

    for d in (1, 3, 2):
        c = (my_x + d) % X
        sent(recv_q.at[c], q_recv.at[c])
    sent(recv_b, b_recv)

    @pl.loop(0, GROUP)
    def _(i):
        unpack(recv_q[i // 4, i % 4], q_extra, pl.multiple_of(i * W, W))

    lanes_q = lanes_of((QB, LANES))

    def extra_queries(n):
        c = (my_x + n + 1) % X
        return q_extra[pl.ds(pl.multiple_of(c * QB, QB), QB)]

    def extra_done(n, top, out):
        total = out[:, 0:1]
        hi, mid, lo = thirds(top + jnp.log(total))
        lse = jnp.where(lanes_q < 16, hi, jnp.where(lanes_q < 32, mid, lo))
        packed = jnp.where(lanes_q < HEAD_DIM, lse, out / total).astype(BF16)
        if n < X - 1:
            part_tx[n] = packed
            pltpu.make_async_remote_copy(
                part_tx.at[n], part_rx.at[my_x], p_send.at[n], p_recv, device_id=at(my_y, (my_x + n + 1) % X, my_z)
            ).start()
        else:
            part_rx[my_x] = packed

    attend(recv_b[...].reshape(KEYS, LANES), extra_queries, None, None, extra_done)
    main_step(3)

    def pack_rows(out, r):
        top, bottom = out[r * W : r * W + 32], out[r * W + 32 : (r + 1) * W]
        return jnp.where(left_half, rolled(top), bottom).astype(BF16)

    def home(slot, i, head):
        y, z = i // Z, i % Z

        @pl.when(i == my_i)
        def _():
            pltpu.make_async_copy(o_tx.at[slot], o_rx.at[my_y, head], o_recv).start()

        @pl.when(i != my_i)
        def _():
            pltpu.make_async_remote_copy(
                o_tx.at[slot], o_rx.at[my_y, head], o_send, o_recv, device_id=at(y, my_x, z)
            ).start()

    last = (my_x + 2) % X
    sent(kvx.at[last], f_recv.at[last])

    def main_done(n, top, out):
        out = out / out[:, 0:1]
        for r in range(QB // W):
            o_tx[n * (QB // W) + r] = pack_rows(out, r)
        for r in range(QB // W):
            home(n * (QB // W) + r, n * (QB // W) + r, my_z)

    attend(keys_of(last), main_queries, main_tops, main_sums, main_done)

    sent(part_rx.at[pl.ds(0, X - 1)], p_recv)
    parts = [part_rx[c].astype(F32) for c in range(X)]
    lses = [p[:, 0:1] + p[:, 16:17] + p[:, 32:33] for p in parts]
    peak = functools.reduce(jnp.maximum, lses)
    weights = [jnp.exp(lse - peak) for lse in lses]
    merged = sum(w * p for w, p in zip(weights, parts)) / sum(weights)
    for r in range(4):
        o_tx[GROUP + r] = pack_rows(merged, r)
    for r in range(4):
        quarter = my_z % 4
        home(GROUP + r, (r // 2) * Z + quarter * 2 + r % 2, Z + my_z // 4)

    sent(o_rx, o_recv)
    for b in range(IMAGES):
        for j in range(HEADS // 2):
            even, odd = o_rx[b, 2 * j].astype(F32), o_rx[b, 2 * j + 1].astype(F32)
            att[b * W : b * W + 32, j * LANES : (j + 1) * LANES] = jnp.where(left_half, even, rolled(odd)).astype(BF16)
            att[b * W + 32 : (b + 1) * W, j * LANES : (j + 1) * LANES] = jnp.where(
                left_half, rolled(even), odd
            ).astype(BF16)
    loads[5].wait()
    mixed = jnp.dot(att[...], wo[...], preferred_element_type=F32)
    fresh_s[...] = (resid_s[...].astype(F32) + mixed).astype(BF16).reshape(IMAGES, W, C)
    pass_on = pltpu.make_async_remote_copy(
        fresh_s, handed_hbm.at[0, :, 0], h_send, h_recv, device_id={"section": (sec + 1) % 4}
    )
    pass_on.start()
    keep_copy = pltpu.make_async_copy(fresh_s, fresh_hbm.at[0, :, 0], out_sem)
    keep_copy.start()

    below.wait_send()
    above.wait_send()
    sent(three, st_send.at[1])
    sent(recv_a.at[pl.ds(0, GROUP - 1)], a_send)
    sent(recv_b.at[pl.ds(0, GROUP - 1)], b_send)
    for b in range(IMAGES):
        for e in range(2):
            here = (my_z // 2 + 4 * e == my_z) & (my_y == b)

            @pl.when(jnp.logical_not(here))
            def _():
                sent(send_q.at[b, e], q_send.at[b * 2 + e])

    sent(kvx.at[pl.ds(0, X - 1)], f_send)
    sent(recv_q.at[pl.ds(0, X - 1)], qf_send)
    for t in range(X - 1):
        sent(part_tx.at[t], p_send.at[t])
    at_home = (my_z % 4) == (my_z // 2)

    @pl.when(at_home)
    def _():
        sent(o_tx.at[pl.ds(0, GROUP + 4 - 2)], o_send)

    @pl.when(jnp.logical_not(at_home))
    def _():
        sent(o_tx.at[pl.ds(0, GROUP + 4 - 1)], o_send)

    keep_copy.wait()
    pass_on.wait()


def body(*args):
    hbm = pl.BlockSpec(memory_space=pltpu.HBM)
    out = jax.ShapeDtypeStruct((1, IMAGES, 1, W, C), BF16)
    dma = pltpu.SemaphoreType.DMA
    return pl.pallas_call(
        kernel,
        out_shape=(out, out),
        in_specs=[hbm] * 13,
        out_specs=(hbm, hbm),
        scratch_shapes=[
            pltpu.SMEM((1,), jnp.int32),
            pltpu.VMEM((5, 1, C), F32),
            pltpu.VMEM((3, IMAGES, W, C), BF16),
            pltpu.VMEM((3, 3, C, C), BF16),
            pltpu.VMEM((TEMB, C), BF16),
            pltpu.VMEM((C, C), BF16),
            pltpu.VMEM((C, C), BF16),
            pltpu.VMEM((C, C), BF16),
            pltpu.VMEM((C, C), BF16),
            pltpu.VMEM((8, LANES), F32),
            pltpu.VMEM((GROUP, 8, LANES), F32),
            pltpu.VMEM((X, 8, LANES), F32),
            pltpu.VMEM((IMAGES, 3, W + 16, C), F32),
            pltpu.VMEM((IMAGES * W, 9 * C), BF16),
            pltpu.VMEM((IMAGES * W, C), BF16),
            pltpu.VMEM((IMAGES, Z, 96, LANES), BF16),
            pltpu.VMEM((IMAGES, 2, W, LANES), BF16),
            pltpu.VMEM((IMAGES, 2, W // 2, LANES), BF16),
            pltpu.VMEM((GROUP, 96, LANES), BF16),
            pltpu.VMEM((GROUP, W, LANES), BF16),
            pltpu.VMEM((X, 4, W // 2, LANES), BF16),
            pltpu.VMEM((X, GROUP, W, LANES), BF16),
            pltpu.VMEM((KEYS, LANES), BF16),
            pltpu.VMEM((KEYS, LANES), BF16),
            pltpu.VMEM((KEYS, LANES), F32),
            pltpu.VMEM((KEYS, LANES), F32),
            pltpu.VMEM((X - 1, QB, LANES), BF16),
            pltpu.VMEM((X, QB, LANES), BF16),
            pltpu.VMEM((GROUP + 4, W // 2, LANES), BF16),
            pltpu.VMEM((IMAGES, HEADS, W // 2, LANES), BF16),
            pltpu.VMEM((IMAGES * W, C), BF16),
            pltpu.VMEM((IMAGES, W, C), BF16),
            dma,
            dma((6,)),
            dma((2,)),
            dma((2,)),
            dma((2,)),
            dma((2,)),
            dma,
            dma((GROUP,)),
            dma,
            dma,
            dma((4,)),
            dma((X,)),
            dma,
            dma((X,)),
            dma,
            dma((X - 1,)),
            dma,
            dma,
            dma,
            dma,
            dma,
            dma,
            dma((6,)),
        ],
        compiler_params=pltpu.CompilerParams(
            collective_id=0, has_side_effects=True, vmem_limit_bytes=63 * 1024 * 1024
        ),
    )(*args)


def solution(mesh):
    placed = (
        P(),
        P("section", None, "patch", None, None),
        P("section", None, None, None, None),
        P("section", None),
        P("section", None),
        P("section", None),
        P("section", None, None),
        P("section", None),
        P("section", None),
        P("section", None, None),
        P("section", None, None),
        P("section", None, None),
        P("section", None, None),
    )
    whole = P("section", None, "patch", None, None)
    return jax.shard_map(body, mesh=mesh, in_specs=placed, out_specs=(whole, whole), check_vma=False)
```

profile of v0, /device:TPU:1, one launch (start us, length us, event | category | flops | bytes accessed | tf_op | source)
XLA Modules:
  0.0 63.8 jit_solution(5962220239958115351)
XLA Ops:
  1.3 59.3 %shard_map.140 = (bf16[1,2,1,64,640]{4,3,2,1,0:T(8,128)(2,1)}, bf16[1,2,1,64,640]{4,3,2,1,0:T(8,128)(2,1)}) custom-call(s32[1]{0:T(128)S(6)} %copy.17.ts_hbm, bf16[1,2,1,64,640]{4,3,2,1,0:T(8,128)(2,1)} %x_hbm.1, bf16[1,3,3,640,640]{4,3,2,1,0:T(8,128)(2,1)} %ck_hbm.1, f32[1,640]{1,0:T(1,128)} %cb_hbm.1, f32[1,640]{1,0:T(1,128)} %gg_hbm.1, f32[1,640]{1,0:T(1,128)} %gb_hbm.1, ...), custom_call_target="tpu_custom_call" | custom-call | tf_op jit(solution)/shard_map/pallas_call | solution.py:486
  60.6 1.6 %copy.18 = bf16[1,2,1,64,640]{4,3,2,1,0:T(8,128)(2,1)} copy(bf16[1,2,1,64,640]{4,3,2,1,0:T(8,128)(2,1)} %get-tuple-element.4) | data formatting | bytes 327680
  62.2 1.6 %copy.19 = bf16[1,2,1,64,640]{4,3,2,1,0:T(8,128)(2,1)} copy(bf16[1,2,1,64,640]{4,3,2,1,0:T(8,128)(2,1)} %get-tuple-element.5) | data formatting | bytes 327680
where the time goes:
time: 63.9 us; the launch traced here: 63.8 us
  Pallas kernels  59.3 us (93%)
  local copies, waits for them, and re-layouts  3.19 us (5%)
  between operations  1.29 us (2%)
    pallas_call x1, Pallas kernels, body(): pl.pallas_call(kernel, out_shape=(out, out), in_specs=[hbm] * 13, out_spe...  59.3 us
    unnamed x2, local copies, waits for them, and re-layouts  3.19 us

commit v1 on v0

--- a/solution.py
+++ b/solution.py
@@ -50,13 +50,13 @@
 
 def kernel(
     ts_hbm, x_hbm, ck_hbm, cb_hbm, gg_hbm, gb_hbm, tw_hbm, ng_hbm, nb_hbm, wq_hbm, wk_hbm, wv_hbm, wo_hbm,
-    fresh_hbm, handed_hbm,
+    out_hbm,
     ts_ref, vectors, xin, wc, wt, wq, wk, wv, wo,
     stat_tx, stat_rx, stat2_rx, pad, patches, resid_s,
-    send_a, send_b, send_q, recv_a, recv_b, recv_q, kvx, q_main, q_extra,
+    send_kv, send_qm, send_b, send_q, recv_kv, recv_qm, recv_b, recv_q, kvx, q_main, q_extra,
     m_s, acc_s, part_tx, part_rx, o_tx, o_rx, att, fresh_s,
     x_sem, w_sem, st_send, st_recv, halo_send, halo_recv,
-    a_send, a_recv, b_send, b_recv, q_send, q_recv, f_send, f_recv, qf_send, p_send, p_recv, o_send, o_recv,
+    a_send, a_recv, qm_recv, b_send, b_recv, q_send, q_recv, f_send, f_recv, qf_send, p_send, p_recv, o_send, o_recv,
     out_sem, h_send, h_recv, v_sem,
 ):
     me = lax.axis_index("patch")
@@ -87,7 +87,7 @@
         for n, ref in enumerate((cb_hbm, gg_hbm, gb_hbm, ng_hbm, nb_hbm))
     ]
     small.append(pltpu.make_async_copy(ts_hbm, ts_ref, v_sem.at[5]))
-    for load in [*small, *loads]:
+    for load in [*small, loads[0]]:
         load.start()
 
     barrier = pltpu.get_barrier_semaphore()
@@ -140,6 +140,9 @@
     below.start()
     above.start()
 
+    for load in loads[1:]:
+        load.start()
+
     half = TEMB // 2
     place = lax.broadcasted_iota(jnp.int32, (8, TEMB), 1)
     step = jnp.where(place < half, place, place - half).astype(F32)
@@ -155,7 +158,6 @@
     sent(fifteen, st_recv.at[0])
     column_stats = jnp.sum(stat_rx[...], axis=0)
     stat2_rx[my_x] = column_stats
-    sent(fifteen, st_send.at[0])
     for k in (1, 3, 2):
         pltpu.make_async_remote_copy(
             stat2_rx.at[my_x], stat2_rx.at[my_x], st_send.at[1], st_recv.at[1],
@@ -214,11 +216,11 @@
             for e in range(2):
                 head = 2 * j + e
                 if head < Z:
-                    send_a[b, head, 0:32] = qq[e].astype(BF16)
-                    send_a[b, head, 32:96] = kv[e].astype(BF16)
+                    send_qm[b, head] = qq[e].astype(BF16)
+                    send_kv[b, head] = kv[e].astype(BF16)
                 else:
-                    send_q[b, head - Z] = qq[e].astype(BF16)
-                    send_b[b, head - Z] = kv[e].astype(BF16)
+                    send_q[b * 2 + head - Z] = qq[e].astype(BF16)
+                    send_b[b * 2 + head - Z] = kv[e].astype(BF16)
 
     def partner(k):
         m = k // 2
@@ -226,65 +228,48 @@
         dz = odd * ((m + 1) // 2) + (1 - odd) * ((Z - m // 2) % Z)
         return (my_y + k % 2) % 2, dz
 
-    @pl.loop(0, GROUP)
-    def _(k):
+    def to_group(k, source, target, send_sem, recv_sem):
         b, dz = partner(k)
         z = (my_z + dz) % Z
 
         @pl.when(k == 0)
         def _():
-            pltpu.make_async_copy(send_a.at[b, z], recv_a.at[my_i], a_recv.at[my_i]).start()
+            pltpu.make_async_copy(source(b, z), target, recv_sem).start()
 
         @pl.when(k > 0)
         def _():
             pltpu.make_async_remote_copy(
-                send_a.at[b, z], recv_a.at[my_i], a_send, a_recv.at[my_i], device_id=at(b, my_x, z)
+                source(b, z), target, send_sem, recv_sem, device_id=at(b, my_x, z)
             ).start()
 
-    member = my_y * 2 + my_z % 2
-    for b in range(IMAGES):
-        for e in range(2):
-            z = my_z // 2 + 4 * e
-            here = (z == my_z) & (my_y == b)
-
-            @pl.when(here)
-            def _():
-                pltpu.make_async_copy(send_q.at[b, e], recv_q.at[my_x, member], q_recv.at[my_x]).start()
-
-            @pl.when(jnp.logical_not(here))
-            def _():
-                pltpu.make_async_remote_copy(
-                    send_q.at[b, e], recv_q.at[my_x, member], q_send.at[b * 2 + e], q_recv.at[my_x],
-                    device_id=at(b, my_x, z),
-                ).start()
+    own_pair = my_z // 2
+    for d in range(4):
+        pair = (own_pair + d) % 4
+        source, target = send_q.at[pair], recv_q.at[my_x, own_pair]
+        if d == 0:
+            pltpu.make_async_copy(source, target, q_recv.at[my_x]).start()
+        else:
+            pltpu.make_async_remote_copy(
+                source, target, q_send, q_recv.at[my_x], device_id=at(my_y, my_x, 2 * pair + my_z % 2)
+            ).start()
+
+    pltpu.make_async_copy(send_b.at[own_pair], recv_b.at[my_y, my_z], b_recv.at[0]).start()
+
+    @pl.loop(1, Z)
+    def _(k):
+        odd = k % 2
+        z = (my_z + odd * ((k + 1) // 2) + (1 - odd) * (Z - k // 2)) % Z
+        pltpu.make_async_remote_copy(
+            send_b.at[z // 2], recv_b.at[my_y, my_z], b_send.at[0], b_recv.at[0], device_id=at(my_y, my_x, z)
+        ).start()
 
     @pl.loop(0, GROUP)
     def _(k):
-        b, dz = partner(k)
-        z = (my_z + dz) % Z
-
-        @pl.when(k == 0)
-        def _():
-            pltpu.make_async_copy(send_b.at[b, z // 4], recv_b.at[my_i], b_recv).start()
-
-        @pl.when(k > 0)
-        def _():
-            pltpu.make_async_remote_copy(
-                send_b.at[b, z // 4], recv_b.at[my_i], b_send, b_recv, device_id=at(b, my_x, z)
-            ).start()
+        to_group(k, lambda b, z: send_kv.at[b, z], recv_kv.at[my_i], a_send.at[0], a_recv.at[my_i])
 
     @pl.loop(0, GROUP)
     def _(k):
-        y, dz = partner(k)
-        z = (my_z + Z - dz) % Z
-        i = y * Z + z
-        sent(recv_a.at[i], a_recv.at[i])
-        chunk = recv_a.at[i, pl.ds(32, W)]
-        pltpu.make_async_copy(chunk, kvx.at[my_x, i], f_recv.at[my_x]).start()
-        for d in (1, 3, 2):
-            pltpu.make_async_remote_copy(
-                chunk, kvx.at[my_x, i], f_send, f_recv.at[my_x], device_id=at(my_y, (my_x + d) % X, my_z)
-            ).start()
+        to_group(k, lambda b, z: send_qm.at[b, z], recv_qm.at[my_i], a_send.at[1], qm_recv)
 
     sent(recv_q.at[my_x], q_recv.at[my_x])
     for d in (1, 3, 2):
@@ -292,15 +277,27 @@
             recv_q.at[my_x], recv_q.at[my_x], qf_send, q_recv.at[my_x],
             device_id=at(my_y, (my_x + d) % X, my_z),
         ).start()
+    sent(recv_b.at[my_y], b_recv.at[0])
+    across = pltpu.make_async_remote_copy(
+        recv_b.at[my_y], recv_b.at[my_y], b_send.at[1], b_recv.at[1], device_id=at(1 - my_y, my_x, my_z)
+    )
+    across.start()
+
+    @pl.loop(0, GROUP)
+    def _(k):
+        y, dz = partner(k)
+        z = (my_z + Z - dz) % Z
+        i = y * Z + z
+        sent(recv_kv.at[i], a_recv.at[i])
+        for d in (1, 3, 2):
+            pltpu.make_async_remote_copy(
+                recv_kv.at[i], kvx.at[d - 1, i], f_send, f_recv.at[d - 1], device_id=at(my_y, (my_x + d) % X, my_z)
+            ).start()
 
     def unpack(packed, out, base):
         wide = packed.astype(F32)
         out[pl.ds(base, 32)] = jnp.where(left_half, wide, 0.0).astype(BF16)
         out[pl.ds(base + 32, 32)] = jnp.where(left_half, rolled(wide), 0.0).astype(BF16)
-
-    @pl.loop(0, GROUP)
-    def _(i):
-        unpack(recv_a[i, 0:32], q_main, pl.multiple_of(i * W, W))
 
     def rows_of(n):
         return slice(n * QB, (n + 1) * QB)
@@ -332,9 +329,6 @@
             done(n, top, out)
             score = following
 
-    def keys_of(c):
-        return kvx[c].reshape(KEYS, LANES)
-
     def main_queries(n):
         return q_main[rows_of(n)]
 
@@ -348,20 +342,10 @@
         m_s[rows_of(n)] = top
         acc_s[rows_of(n)] = out
 
-    sent(kvx.at[my_x], f_recv.at[my_x])
-    attend(keys_of(my_x), main_queries, None, None, keep_main)
-
-    def main_step(d):
-        c = (my_x + d) % X
-        sent(kvx.at[c], f_recv.at[c])
-        attend(keys_of(c), main_queries, main_tops, main_sums, keep_main)
-
-    main_step(1)
-
     for d in (1, 3, 2):
         c = (my_x + d) % X
         sent(recv_q.at[c], q_recv.at[c])
-    sent(recv_b, b_recv)
+    sent(recv_b.at[my_y], b_recv.at[1])
 
     @pl.loop(0, GROUP)
     def _(i):
@@ -387,36 +371,34 @@
             part_rx[my_x] = packed
 
     attend(recv_b[...].reshape(KEYS, LANES), extra_queries, None, None, extra_done)
-    main_step(3)
+
+    sent(recv_qm, qm_recv)
+
+    @pl.loop(0, GROUP)
+    def _(i):
+        unpack(recv_qm[i], q_main, pl.multiple_of(i * W, W))
+
+    attend(recv_kv[...].reshape(KEYS, LANES), main_queries, None, None, keep_main)
+    for d in (1, 3):
+        sent(kvx.at[d - 1], f_recv.at[d - 1])
+        attend(kvx[d - 1].reshape(KEYS, LANES), main_queries, main_tops, main_sums, keep_main)
 
     def pack_rows(out, r):
         top, bottom = out[r * W : r * W + 32], out[r * W + 32 : (r + 1) * W]
         return jnp.where(left_half, rolled(top), bottom).astype(BF16)
 
-    def home(slot, i, head):
+    def home(slot, i, image, head):
         y, z = i // Z, i % Z
 
         @pl.when(i == my_i)
         def _():
-            pltpu.make_async_copy(o_tx.at[slot], o_rx.at[my_y, head], o_recv).start()
+            pltpu.make_async_copy(o_tx.at[slot], o_rx.at[image, head], o_recv).start()
 
         @pl.when(i != my_i)
         def _():
             pltpu.make_async_remote_copy(
-                o_tx.at[slot], o_rx.at[my_y, head], o_send, o_recv, device_id=at(y, my_x, z)
+                o_tx.at[slot], o_rx.at[image, head], o_send, o_recv, device_id=at(y, my_x, z)
             ).start()
-
-    last = (my_x + 2) % X
-    sent(kvx.at[last], f_recv.at[last])
-
-    def main_done(n, top, out):
-        out = out / out[:, 0:1]
-        for r in range(QB // W):
-            o_tx[n * (QB // W) + r] = pack_rows(out, r)
-        for r in range(QB // W):
-            home(n * (QB // W) + r, n * (QB // W) + r, my_z)
-
-    attend(keys_of(last), main_queries, main_tops, main_sums, main_done)
 
     sent(part_rx.at[pl.ds(0, X - 1)], p_recv)
     parts = [part_rx[c].astype(F32) for c in range(X)]
@@ -427,8 +409,18 @@
     for r in range(4):
         o_tx[GROUP + r] = pack_rows(merged, r)
     for r in range(4):
-        quarter = my_z % 4
-        home(GROUP + r, (r // 2) * Z + quarter * 2 + r % 2, Z + my_z // 4)
+        home(GROUP + r, my_y * Z + 2 * r + my_z % 2, my_z // 4, Z + own_pair % 2)
+
+    sent(kvx.at[1], f_recv.at[1])
+
+    def main_done(n, top, out):
+        out = out / out[:, 0:1]
+        for r in range(QB // W):
+            o_tx[n * (QB // W) + r] = pack_rows(out, r)
+        for r in range(QB // W):
+            home(n * (QB // W) + r, n * (QB // W) + r, my_y, my_z)
+
+    attend(kvx[1].reshape(KEYS, LANES), main_queries, main_tops, main_sums, main_done)
 
     sent(o_rx, o_recv)
     for b in range(IMAGES):
@@ -442,52 +434,39 @@
     mixed = jnp.dot(att[...], wo[...], preferred_element_type=F32)
     fresh_s[...] = (resid_s[...].astype(F32) + mixed).astype(BF16).reshape(IMAGES, W, C)
     pass_on = pltpu.make_async_remote_copy(
-        fresh_s, handed_hbm.at[0, :, 0], h_send, h_recv, device_id={"section": (sec + 1) % 4}
+        fresh_s, out_hbm.at[1], h_send, h_recv, device_id={"section": (sec + 1) % 4}
     )
     pass_on.start()
-    keep_copy = pltpu.make_async_copy(fresh_s, fresh_hbm.at[0, :, 0], out_sem)
+    keep_copy = pltpu.make_async_copy(fresh_s, out_hbm.at[0], out_sem)
     keep_copy.start()
 
     below.wait_send()
     above.wait_send()
+    sent(fifteen, st_send.at[0])
     sent(three, st_send.at[1])
-    sent(recv_a.at[pl.ds(0, GROUP - 1)], a_send)
-    sent(recv_b.at[pl.ds(0, GROUP - 1)], b_send)
-    for b in range(IMAGES):
-        for e in range(2):
-            here = (my_z // 2 + 4 * e == my_z) & (my_y == b)
-
-            @pl.when(jnp.logical_not(here))
-            def _():
-                sent(send_q.at[b, e], q_send.at[b * 2 + e])
-
-    sent(kvx.at[pl.ds(0, X - 1)], f_send)
+    sent(recv_kv.at[pl.ds(0, GROUP - 1)], a_send.at[0])
+    sent(recv_qm.at[pl.ds(0, GROUP - 1)], a_send.at[1])
+    sent(recv_b.at[0, pl.ds(0, Z - 1)], b_send.at[0])
+    across.wait_send()
+    sent(send_q.at[pl.ds(0, 3)], q_send)
+    sent(kvx, f_send)
     sent(recv_q.at[pl.ds(0, X - 1)], qf_send)
     for t in range(X - 1):
         sent(part_tx.at[t], p_send.at[t])
-    at_home = (my_z % 4) == (my_z // 2)
-
-    @pl.when(at_home)
-    def _():
-        sent(o_tx.at[pl.ds(0, GROUP + 4 - 2)], o_send)
-
-    @pl.when(jnp.logical_not(at_home))
-    def _():
-        sent(o_tx.at[pl.ds(0, GROUP + 4 - 1)], o_send)
-
+    sent(o_tx.at[pl.ds(0, GROUP + 4 - 2)], o_send)
     keep_copy.wait()
     pass_on.wait()
 
 
 def body(*args):
     hbm = pl.BlockSpec(memory_space=pltpu.HBM)
-    out = jax.ShapeDtypeStruct((1, IMAGES, 1, W, C), BF16)
+    out = jax.ShapeDtypeStruct((2, IMAGES, W, C), BF16)
     dma = pltpu.SemaphoreType.DMA
-    return pl.pallas_call(
+    both = pl.pallas_call(
         kernel,
-        out_shape=(out, out),
+        out_shape=out,
         in_specs=[hbm] * 13,
-        out_specs=(hbm, hbm),
+        out_specs=hbm,
         scratch_shapes=[
             pltpu.SMEM((1,), jnp.int32),
             pltpu.VMEM((5, 1, C), F32),
@@ -504,13 +483,15 @@
             pltpu.VMEM((IMAGES, 3, W + 16, C), F32),
             pltpu.VMEM((IMAGES * W, 9 * C), BF16),
             pltpu.VMEM((IMAGES * W, C), BF16),
-            pltpu.VMEM((IMAGES, Z, 96, LANES), BF16),
-            pltpu.VMEM((IMAGES, 2, W, LANES), BF16),
-            pltpu.VMEM((IMAGES, 2, W // 2, LANES), BF16),
-            pltpu.VMEM((GROUP, 96, LANES), BF16),
+            pltpu.VMEM((IMAGES, Z, W, LANES), BF16),
+            pltpu.VMEM((IMAGES, Z, W // 2, LANES), BF16),
+            pltpu.VMEM((4, W, LANES), BF16),
+            pltpu.VMEM((4, W // 2, LANES), BF16),
             pltpu.VMEM((GROUP, W, LANES), BF16),
+            pltpu.VMEM((GROUP, W // 2, LANES), BF16),
+            pltpu.VMEM((2, Z, W, LANES), BF16),
             pltpu.VMEM((X, 4, W // 2, LANES), BF16),
-            pltpu.VMEM((X, GROUP, W, LANES), BF16),
+            pltpu.VMEM((X - 1, GROUP, W, LANES), BF16),
             pltpu.VMEM((KEYS, LANES), BF16),
             pltpu.VMEM((KEYS, LANES), BF16),
             pltpu.VMEM((KEYS, LANES), F32),
@@ -527,14 +508,15 @@
             dma((2,)),
             dma((2,)),
             dma((2,)),
-            dma,
+            dma((2,)),
             dma((GROUP,)),
             dma,
-            dma,
-            dma((4,)),
+            dma((2,)),
+            dma((2,)),
+            dma,
             dma((X,)),
             dma,
-            dma((X,)),
+            dma((X - 1,)),
             dma,
             dma((X - 1,)),
             dma,
@@ -549,6 +531,8 @@
             collective_id=0, has_side_effects=True, vmem_limit_bytes=63 * 1024 * 1024
         ),
     )(*args)
+    whole = (1, IMAGES, 1, W, C)
+    return both[0].reshape(whole), both[1].reshape(whole)
 
 
 def solution(mesh):

time: 63.9 us -> 58.5 us (0.915)
  Pallas kernels: 59.3 us -> 55.4 us
  local copies, waits for them, and re-layouts: 3.19 us -> 1.75 us
    pallas_call x1, Pallas kernels: 59.3 us -> 55.4 us  [body(): pl.pallas_call(kernel, out_shape=out, in_specs=[hbm] * 13, out_specs=hbm,...]
    unnamed x2 -> x1, local copies, waits for them, and re-layouts: 3.19 us -> 1.75 us
where the time goes in v1:
time: 58.5 us; the launch traced here: 58.4 us
  Pallas kernels  55.4 us (95%)
  local copies, waits for them, and re-layouts  1.75 us (3%)
  between operations  1.29 us (2%)
    pallas_call x1, Pallas kernels, body(): pl.pallas_call(kernel, out_shape=out, in_specs=[hbm] * 13, out_specs=hbm,...  55.4 us
    unnamed x1, local copies, waits for them, and re-layouts  1.75 us

profile of v1, /device:TPU:1, one launch (start us, length us, event | category | flops | bytes accessed | tf_op | source)
XLA Modules:
  0.0 58.4 jit_solution(15269826229650637028)
XLA Ops:
  1.3 55.4 %shard_map.140 = bf16[2,2,64,640]{3,2,1,0:T(8,128)(2,1)} custom-call(s32[1]{0:T(128)S(6)} %copy.17.ts_hbm, bf16[1,2,1,64,640]{4,3,2,1,0:T(8,128)(2,1)} %x_hbm.1, bf16[1,3,3,640,640]{4,3,2,1,0:T(8,128)(2,1)} %ck_hbm.1, f32[1,640]{1,0:T(1,128)} %cb_hbm.1, f32[1,640]{1,0:T(1,128)} %gg_hbm.1, f32[1,640]{1,0:T(1,128)} %gb_hbm.1, bf16[1,320,640]{2,1,0:T(8,128)(2,1)} %tw_hbm.1, ...), custom_call_target="tpu_custom_call" | custom-call | tf_op jit(solution)/shard_map/pallas_call | solution.py:465
  56.7 1.7 %slice_bitcast_fusion = (bf16[1,2,1,64,640]{4,3,2,1,0:T(8,128)(2,1)}, bf16[1,2,1,64,640]{4,3,2,1,0:T(8,128)(2,1)}) fusion(bf16[2,2,64,640]{3,2,1,0:T(8,128)(2,1)} %shard_map.140), kind=kLoop, calls=%fused_computation | loop fusion | bytes 655360

commit v2 on v1

--- a/solution.py
+++ b/solution.py
@@ -342,6 +342,14 @@
         m_s[rows_of(n)] = top
         acc_s[rows_of(n)] = out
 
+    sent(recv_qm, qm_recv)
+
+    @pl.loop(0, GROUP)
+    def _(i):
+        unpack(recv_qm[i], q_main, pl.multiple_of(i * W, W))
+
+    attend(recv_kv[...].reshape(KEYS, LANES), main_queries, None, None, keep_main)
+
     for d in (1, 3, 2):
         c = (my_x + d) % X
         sent(recv_q.at[c], q_recv.at[c])
@@ -372,13 +380,6 @@
 
     attend(recv_b[...].reshape(KEYS, LANES), extra_queries, None, None, extra_done)
 
-    sent(recv_qm, qm_recv)
-
-    @pl.loop(0, GROUP)
-    def _(i):
-        unpack(recv_qm[i], q_main, pl.multiple_of(i * W, W))
-
-    attend(recv_kv[...].reshape(KEYS, LANES), main_queries, None, None, keep_main)
     for d in (1, 3):
         sent(kvx.at[d - 1], f_recv.at[d - 1])
         attend(kvx[d - 1].reshape(KEYS, LANES), main_queries, main_tops, main_sums, keep_main)

time: 58.5 us -> 59.8 us (1.022)
  Pallas kernels: 55.4 us -> 56.6 us
    pallas_call x1, Pallas kernels: 55.4 us -> 56.6 us  [body(): pl.pallas_call(kernel, out_shape=out, in_specs=[hbm] * 13, out_specs=hbm,...]
where the time goes in v2:
time: 59.8 us; the launch traced here: 59.7 us
  Pallas kernels  56.6 us (95%)
  local copies, waits for them, and re-layouts  1.75 us (3%)
  between operations  1.29 us (2%)
    pallas_call x1, Pallas kernels, body(): pl.pallas_call(kernel, out_shape=out, in_specs=[hbm] * 13, out_specs=hbm,...  56.6 us
    unnamed x1, local copies, waits for them, and re-layouts  1.75 us

profile of v2, /device:TPU:1, one launch (start us, length us, event | category | flops | bytes accessed | tf_op | source)
XLA Modules:
  0.0 59.7 jit_solution(5183508846321883030)
XLA Ops:
  1.3 56.6 %shard_map.140 = bf16[2,2,64,640]{3,2,1,0:T(8,128)(2,1)} custom-call(s32[1]{0:T(128)S(6)} %copy.17.ts_hbm, bf16[1,2,1,64,640]{4,3,2,1,0:T(8,128)(2,1)} %x_hbm.1, bf16[1,3,3,640,640]{4,3,2,1,0:T(8,128)(2,1)} %ck_hbm.1, f32[1,640]{1,0:T(1,128)} %cb_hbm.1, f32[1,640]{1,0:T(1,128)} %gg_hbm.1, f32[1,640]{1,0:T(1,128)} %gb_hbm.1, bf16[1,320,640]{2,1,0:T(8,128)(2,1)} %tw_hbm.1, ...), custom_call_target="tpu_custom_call" | custom-call | tf_op jit(solution)/shard_map/pallas_call | solution.py:466
  57.9 1.7 %slice_bitcast_fusion = (bf16[1,2,1,64,640]{4,3,2,1,0:T(8,128)(2,1)}, bf16[1,2,1,64,640]{4,3,2,1,0:T(8,128)(2,1)}) fusion(bf16[2,2,64,640]{3,2,1,0:T(8,128)(2,1)} %shard_map.140), kind=kLoop, calls=%fused_computation | loop fusion | bytes 655360

commit v3 on v1

--- a/solution.py
+++ b/solution.py
@@ -400,6 +400,17 @@
                 o_tx.at[slot], o_rx.at[image, head], o_send, o_recv, device_id=at(y, my_x, z)
             ).start()
 
+    sent(kvx.at[1], f_recv.at[1])
+
+    def main_done(n, top, out):
+        out = out / out[:, 0:1]
+        for r in range(QB // W):
+            o_tx[n * (QB // W) + r] = pack_rows(out, r)
+        for r in range(QB // W):
+            home(n * (QB // W) + r, n * (QB // W) + r, my_y, my_z)
+
+    attend(kvx[1].reshape(KEYS, LANES), main_queries, main_tops, main_sums, main_done)
+
     sent(part_rx.at[pl.ds(0, X - 1)], p_recv)
     parts = [part_rx[c].astype(F32) for c in range(X)]
     lses = [p[:, 0:1] + p[:, 16:17] + p[:, 32:33] for p in parts]
@@ -410,17 +421,6 @@
         o_tx[GROUP + r] = pack_rows(merged, r)
     for r in range(4):
         home(GROUP + r, my_y * Z + 2 * r + my_z % 2, my_z // 4, Z + own_pair % 2)
-
-    sent(kvx.at[1], f_recv.at[1])
-
-    def main_done(n, top, out):
-        out = out / out[:, 0:1]
-        for r in range(QB // W):
-            o_tx[n * (QB // W) + r] = pack_rows(out, r)
-        for r in range(QB // W):
-            home(n * (QB // W) + r, n * (QB // W) + r, my_y, my_z)
-
-    attend(kvx[1].reshape(KEYS, LANES), main_queries, main_tops, main_sums, main_done)
 
     sent(o_rx, o_recv)
     for b in range(IMAGES):

time: 58.5 us -> 59.2 us (1.012)
  Pallas kernels: 55.4 us -> 56.1 us
    pallas_call x1, Pallas kernels: 55.4 us -> 56.1 us  [body(): pl.pallas_call(kernel, out_shape=out, in_specs=[hbm] * 13, out_specs=hbm,...]
where the time goes in v3:
time: 59.2 us; the launch traced here: 59.1 us
  Pallas kernels  56.1 us (95%)
  local copies, waits for them, and re-layouts  1.75 us (3%)
  between operations  1.29 us (2%)
    pallas_call x1, Pallas kernels, body(): pl.pallas_call(kernel, out_shape=out, in_specs=[hbm] * 13, out_specs=hbm,...  56.1 us
    unnamed x1, local copies, waits for them, and re-layouts  1.75 us

profile of v3, /device:TPU:1, one launch (start us, length us, event | category | flops | bytes accessed | tf_op | source)
XLA Modules:
  0.0 59.1 jit_solution(10854546194862164606)
XLA Ops:
  1.3 56.1 %shard_map.140 = bf16[2,2,64,640]{3,2,1,0:T(8,128)(2,1)} custom-call(s32[1]{0:T(128)S(6)} %copy.17.ts_hbm, bf16[1,2,1,64,640]{4,3,2,1,0:T(8,128)(2,1)} %x_hbm.1, bf16[1,3,3,640,640]{4,3,2,1,0:T(8,128)(2,1)} %ck_hbm.1, f32[1,640]{1,0:T(1,128)} %cb_hbm.1, f32[1,640]{1,0:T(1,128)} %gg_hbm.1, f32[1,640]{1,0:T(1,128)} %gb_hbm.1, bf16[1,320,640]{2,1,0:T(8,128)(2,1)} %tw_hbm.1, ...), custom_call_target="tpu_custom_call" | custom-call | tf_op jit(solution)/shard_map/pallas_call | solution.py:465
  57.3 1.7 %slice_bitcast_fusion = (bf16[1,2,1,64,640]{4,3,2,1,0:T(8,128)(2,1)}, bf16[1,2,1,64,640]{4,3,2,1,0:T(8,128)(2,1)}) fusion(bf16[2,2,64,640]{3,2,1,0:T(8,128)(2,1)} %shard_map.140), kind=kLoop, calls=%fused_computation | loop fusion | bytes 655360
